TPU v7x, 32 devices: a whole 2x2x4 slice. The times are simulated.
32 devices in a mesh: ang: 8 (over z, core), col: 4 (over y, x).
Axes of the slice: x: 2, y: 2, z: 4, core: 2. Of those that a mesh axis runs over, the one named last changes fastest.
Arguments:
- projections: float32 [512, 16, 4096], P('ang', None, 'col'), may hold values from -6 to 6
- margin: int32 [16], replicated, may hold values from 128 to 384, as said below
- ramp_length: int32 [16], replicated, may hold values from 32 to 128, as said below
Outputs:
- smoothed: float32 [512, 16, 4096], P('ang', None, 'col')
Inputs may be any that keep to these rules, and one draw needn't show every extreme that they name: `margin`: one row has exactly 384 and another exactly 128; other rows may repeat values. `ramp_length`: one row has exactly 128; other rows may repeat values.
All inputs are finite; a program needn't handle non-finite values.
Results may differ from a plain program's by a relative error of at most 0.0003.
Values sent between devices are 32-bit elements; how exact they have to be, the bound alone decides.
A program may use at most 64 MiB of HBM per device.

v0:
```python
import jax
import jax.numpy as jnp
from jax import lax
from jax.sharding import PartitionSpec as P

BAND_MAX = 384
RAMP_MAX = 128
DIFF_STEPS = 6


time_step = 0.2
edge_scale = 0.8


def shifted(value, axis, steps):
    count = lax.axis_size(axis)
    initial, last = (max(0, -steps), min(count, count - steps))
    return lax.ppermute(value, axis, [(source, source + steps) for source in range(initial, last)])


def padded_2(block, sides, width, periodic):
    for axis, dim in sides:
        count = lax.axis_size(axis)
        forward = [(i, i + 1) for i in range(count - 1)]
        if periodic:
            forward.append((count - 1, 0))
        backward = [(target, source) for source, target in forward]
        low = lax.ppermute(
            lax.slice_in_dim(block, block.shape[dim] - width, None, axis=dim), axis, forward
        )
        high = lax.ppermute(lax.slice_in_dim(block, 0, width, axis=dim), axis, backward)
        block = jnp.concatenate([low, block, high], axis=dim)
    return block


def shifted_2(x, axis, by):
    size = lax.axis_size(axis)
    return lax.ppermute(x, axis, [(i, (i + by) % size) for i in range(size)])


def conductive_flux(delta):
    return delta / (1.0 + delta / edge_scale * (delta / edge_scale))


def diffuse_once(current):
    centre_cells = current[1:-1, :, 1:-1]
    summed = conductive_flux(current[:-2, :, 1:-1] - centre_cells) + conductive_flux(
        current[2:, :, 1:-1] - centre_cells
    )
    summed = summed + conductive_flux(current[1:-1, :, :-2] - centre_cells)
    summed = summed + conductive_flux(current[1:-1, :, 2:] - centre_cells)
    return centre_cells + time_step * summed


def shift_rows(source, starts, length):

    def pick_row(row_block, offset):
        return lax.dynamic_slice_in_dim(row_block, offset, length, 1)

    return jax.vmap(pick_row, in_axes=(1, 0), out_axes=1)(source, starts)


def centre_term(source, margin, head_weight):
    reversed_band = source[:, :, ::-1]
    picked = shift_rows(reversed_band, BAND_MAX - margin, RAMP_MAX)
    return (1.0 - head_weight)[None] * picked


def stitch_direct(data, margin, ramp_length, col_index, is_last):
    col_width = data.shape[2]
    leading = data[:, :, :BAND_MAX]
    following = shifted(leading, "col", -1)
    edge_fill = jnp.broadcast_to(data[:, :, col_width - 1 :], following.shape)
    following = jnp.where(is_last, edge_fill, following)
    extended = jnp.concatenate([data, following], axis=2)
    direct = shift_rows(extended, margin, col_width)
    position = (col_index * col_width + jnp.arange(col_width, dtype=jnp.int32)).astype(jnp.float32)
    spread = 2.0 * ramp_length.astype(jnp.float32)
    weight = jnp.minimum(1.0, 0.5 + (position[None, :] + 0.5) / spread[:, None])
    stitched = weight[None] * direct
    head_position = jnp.arange(RAMP_MAX, dtype=jnp.float32)
    head_weight = jnp.minimum(1.0, 0.5 + (head_position[None, :] + 0.5) / spread[:, None])
    return (leading, stitched, head_weight)


def diffuse_round(angle_ext, facing, rim_depth, is_first, is_last):
    col_width = angle_ext.shape[2]
    padded = padded_2(angle_ext, (("col", 2),), rim_depth, False)
    inward = jnp.where(is_first, facing[:, :, ::-1], padded[:, :, :rim_depth])
    reflected = angle_ext[:, :, col_width - rim_depth :][:, :, ::-1]
    outward = jnp.where(is_last, reflected, padded[:, :, -rim_depth:])
    current = jnp.concatenate([inward, angle_ext, outward], axis=2)
    current = diffuse_once(current)
    return current


def per_device(projections, margin, ramp_length):
    col_index = lax.axis_index("col")
    is_first = col_index == 0
    is_last = col_index == lax.axis_size("col") - 1
    half_loop = lax.axis_size("ang") // 2
    leading, stitched, head_weight = stitch_direct(
        projections, margin, ramp_length, col_index, is_last
    )
    partner = shifted_2(leading, "ang", half_loop)
    mirror_add = centre_term(partner, margin, head_weight)
    head_cells = stitched[:, :, :RAMP_MAX] + jnp.where(is_first, mirror_add, 0.0)
    field_now = jnp.concatenate([head_cells, stitched[:, :, RAMP_MAX:]], axis=2)
    rim_depth = 1
    for round_index in range(DIFF_STEPS // rim_depth):
        angle_ext = padded_2(field_now, (("ang", 0),), rim_depth, True)
        facing = shifted_2(angle_ext[:, :, :rim_depth], "ang", half_loop)
        field_now = diffuse_round(angle_ext, facing, rim_depth, is_first, is_last)
    return field_now


def solution(mesh):
    in_specs = (P("ang", None, "col"), P(), P())
    out_specs = P("ang", None, "col")
    return jax.shard_map(
        per_device, mesh=mesh, in_specs=in_specs, out_specs=out_specs, check_vma=False
    )
```

profile of v0, /device:TPU:9, one launch (start us, length us, event | category | flops | bytes accessed | tf_op | source)
XLA Modules:
  0.0 439.5 jit_solution(15719355581329088459)
XLA Ops:
  12.9 60.3 %collective-permute-done.1 = f32[64,16,384]{2,1,0:T(8,128)S(1)} collective-permute-done((f32[64,16,384]{2,1,0:T(8,128)}, f32[64,16,384]{2,1,0:T(8,128)S(1)}, u32[]{:S(2)}, u32[]{:S(2)}) %collective-permute-start.1) | collective-permute-done | bytes 1572896 | tf_op jit(solution)/shard_map/ppermute | solution.py:38
  88.2 149.7 %while.1 = (s32[]{:T(128)}, f32[16,64,1408]{2,1,0:T(8,128)}, s32[16,3]{0,1:T(4,128)S(1)}, f32[16,64,1024]{2,0,1:T(8,128)}, s32[]{:T(128)}, /*index=5*/s32[]{:T(128)}) while((s32[]{:T(128)}, f32[16,64,1408]{2,1,0:T(8,128)}, s32[16,3]{0,1:T(4,128)S(1)}, f32[16,64,1024]{2,0,1:T(8,128)}, s32[]{:T(128)}, /*index=5*/s32[]{:T(128)}) %tuple.31), condition=%wide.while_cond, body=%wide.while_body.sunk | while | flops 2 | bytes 1572997 | solution.py:58
  91.5 6.1 %dynamic-update-slice.3 = f32[16,64,1024]{2,0,1:T(8,128)} dynamic-update-slice(f32[16,64,1024]{2,0,1:T(8,128)} %get-tuple-element.85, f32[1,64,1024]{2,0,1:T(1,128)S(1)} %copy.114, s32[]{:T(128)S(6)} %copy.118, s32[]{:T(128)} %constant.52.clone.1..sunk, s32[]{:T(128)} %constant.52.clone.1..sunk) | dynamic-update-slice | bytes 524292 | tf_op jit(solution)/shard_map/vmap()/gather
  100.9 6.1 %dynamic-update-slice.3 = f32[16,64,1024]{2,0,1:T(8,128)} dynamic-update-slice(f32[16,64,1024]{2,0,1:T(8,128)} %get-tuple-element.85, f32[1,64,1024]{2,0,1:T(1,128)S(1)} %copy.114, s32[]{:T(128)S(6)} %copy.118, s32[]{:T(128)} %constant.52.clone.1..sunk, s32[]{:T(128)} %constant.52.clone.1..sunk) | dynamic-update-slice | bytes 524292 | tf_op jit(solution)/shard_map/vmap()/gather
  110.2 6.1 %dynamic-update-slice.3 = f32[16,64,1024]{2,0,1:T(8,128)} dynamic-update-slice(f32[16,64,1024]{2,0,1:T(8,128)} %get-tuple-element.85, f32[1,64,1024]{2,0,1:T(1,128)S(1)} %copy.114, s32[]{:T(128)S(6)} %copy.118, s32[]{:T(128)} %constant.52.clone.1..sunk, s32[]{:T(128)} %constant.52.clone.1..sunk) | dynamic-update-slice | bytes 524292 | tf_op jit(solution)/shard_map/vmap()/gather
  119.6 6.1 %dynamic-update-slice.3 = f32[16,64,1024]{2,0,1:T(8,128)} dynamic-update-slice(f32[16,64,1024]{2,0,1:T(8,128)} %get-tuple-element.85, f32[1,64,1024]{2,0,1:T(1,128)S(1)} %copy.114, s32[]{:T(128)S(6)} %copy.118, s32[]{:T(128)} %constant.52.clone.1..sunk, s32[]{:T(128)} %constant.52.clone.1..sunk) | dynamic-update-slice | bytes 524292 | tf_op jit(solution)/shard_map/vmap()/gather
  128.9 6.1 %dynamic-update-slice.3 = f32[16,64,1024]{2,0,1:T(8,128)} dynamic-update-slice(f32[16,64,1024]{2,0,1:T(8,128)} %get-tuple-element.85, f32[1,64,1024]{2,0,1:T(1,128)S(1)} %copy.114, s32[]{:T(128)S(6)} %copy.118, s32[]{:T(128)} %constant.52.clone.1..sunk, s32[]{:T(128)} %constant.52.clone.1..sunk) | dynamic-update-slice | bytes 524292 | tf_op jit(solution)/shard_map/vmap()/gather
  138.3 6.1 %dynamic-update-slice.3 = f32[16,64,1024]{2,0,1:T(8,128)} dynamic-update-slice(f32[16,64,1024]{2,0,1:T(8,128)} %get-tuple-element.85, f32[1,64,1024]{2,0,1:T(1,128)S(1)} %copy.114, s32[]{:T(128)S(6)} %copy.118, s32[]{:T(128)} %constant.52.clone.1..sunk, s32[]{:T(128)} %constant.52.clone.1..sunk) | dynamic-update-slice | bytes 524292 | tf_op jit(solution)/shard_map/vmap()/gather
  147.6 6.1 %dynamic-update-slice.3 = f32[16,64,1024]{2,0,1:T(8,128)} dynamic-update-slice(f32[16,64,1024]{2,0,1:T(8,128)} %get-tuple-element.85, f32[1,64,1024]{2,0,1:T(1,128)S(1)} %copy.114, s32[]{:T(128)S(6)} %copy.118, s32[]{:T(128)} %constant.52.clone.1..sunk, s32[]{:T(128)} %constant.52.clone.1..sunk) | dynamic-update-slice | bytes 524292 | tf_op jit(solution)/shard_map/vmap()/gather
  157.0 6.1 %dynamic-update-slice.3 = f32[16,64,1024]{2,0,1:T(8,128)} dynamic-update-slice(f32[16,64,1024]{2,0,1:T(8,128)} %get-tuple-element.85, f32[1,64,1024]{2,0,1:T(1,128)S(1)} %copy.114, s32[]{:T(128)S(6)} %copy.118, s32[]{:T(128)} %constant.52.clone.1..sunk, s32[]{:T(128)} %constant.52.clone.1..sunk) | dynamic-update-slice | bytes 524292 | tf_op jit(solution)/shard_map/vmap()/gather
  166.3 6.1 %dynamic-update-slice.3 = f32[16,64,1024]{2,0,1:T(8,128)} dynamic-update-slice(f32[16,64,1024]{2,0,1:T(8,128)} %get-tuple-element.85, f32[1,64,1024]{2,0,1:T(1,128)S(1)} %copy.114, s32[]{:T(128)S(6)} %copy.118, s32[]{:T(128)} %constant.52.clone.1..sunk, s32[]{:T(128)} %constant.52.clone.1..sunk) | dynamic-update-slice | bytes 524292 | tf_op jit(solution)/shard_map/vmap()/gather
  175.7 6.1 %dynamic-update-slice.3 = f32[16,64,1024]{2,0,1:T(8,128)} dynamic-update-slice(f32[16,64,1024]{2,0,1:T(8,128)} %get-tuple-element.85, f32[1,64,1024]{2,0,1:T(1,128)S(1)} %copy.114, s32[]{:T(128)S(6)} %copy.118, s32[]{:T(128)} %constant.52.clone.1..sunk, s32[]{:T(128)} %constant.52.clone.1..sunk) | dynamic-update-slice | bytes 524292 | tf_op jit(solution)/shard_map/vmap()/gather
  185.0 6.1 %dynamic-update-slice.3 = f32[16,64,1024]{2,0,1:T(8,128)} dynamic-update-slice(f32[16,64,1024]{2,0,1:T(8,128)} %get-tuple-element.85, f32[1,64,1024]{2,0,1:T(1,128)S(1)} %copy.114, s32[]{:T(128)S(6)} %copy.118, s32[]{:T(128)} %constant.52.clone.1..sunk, s32[]{:T(128)} %constant.52.clone.1..sunk) | dynamic-update-slice | bytes 524292 | tf_op jit(solution)/shard_map/vmap()/gather
  194.4 6.1 %dynamic-update-slice.3 = f32[16,64,1024]{2,0,1:T(8,128)} dynamic-update-slice(f32[16,64,1024]{2,0,1:T(8,128)} %get-tuple-element.85, f32[1,64,1024]{2,0,1:T(1,128)S(1)} %copy.114, s32[]{:T(128)S(6)} %copy.118, s32[]{:T(128)} %constant.52.clone.1..sunk, s32[]{:T(128)} %constant.52.clone.1..sunk) | dynamic-update-slice | bytes 524292 | tf_op jit(solution)/shard_map/vmap()/gather
  203.8 6.1 %dynamic-update-slice.3 = f32[16,64,1024]{2,0,1:T(8,128)} dynamic-update-slice(f32[16,64,1024]{2,0,1:T(8,128)} %get-tuple-element.85, f32[1,64,1024]{2,0,1:T(1,128)S(1)} %copy.114, s32[]{:T(128)S(6)} %copy.118, s32[]{:T(128)} %constant.52.clone.1..sunk, s32[]{:T(128)} %constant.52.clone.1..sunk) | dynamic-update-slice | bytes 524292 | tf_op jit(solution)/shard_map/vmap()/gather
  213.1 6.1 %dynamic-update-slice.3 = f32[16,64,1024]{2,0,1:T(8,128)} dynamic-update-slice(f32[16,64,1024]{2,0,1:T(8,128)} %get-tuple-element.85, f32[1,64,1024]{2,0,1:T(1,128)S(1)} %copy.114, s32[]{:T(128)S(6)} %copy.118, s32[]{:T(128)} %constant.52.clone.1..sunk, s32[]{:T(128)} %constant.52.clone.1..sunk) | dynamic-update-slice | bytes 524292 | tf_op jit(solution)/shard_map/vmap()/gather
  222.5 6.1 %dynamic-update-slice.3 = f32[16,64,1024]{2,0,1:T(8,128)} dynamic-update-slice(f32[16,64,1024]{2,0,1:T(8,128)} %get-tuple-element.85, f32[1,64,1024]{2,0,1:T(1,128)S(1)} %copy.114, s32[]{:T(128)S(6)} %copy.118, s32[]{:T(128)} %constant.52.clone.1..sunk, s32[]{:T(128)} %constant.52.clone.1..sunk) | dynamic-update-slice | bytes 524292 | tf_op jit(solution)/shard_map/vmap()/gather
  231.8 6.1 %dynamic-update-slice.3 = f32[16,64,1024]{2,0,1:T(8,128)} dynamic-update-slice(f32[16,64,1024]{2,0,1:T(8,128)} %get-tuple-element.85, f32[1,64,1024]{2,0,1:T(1,128)S(1)} %copy.114, s32[]{:T(128)S(6)} %copy.118, s32[]{:T(128)} %constant.52.clone.1..sunk, s32[]{:T(128)} %constant.52.clone.1..sunk) | dynamic-update-slice | bytes 524292 | tf_op jit(solution)/shard_map/vmap()/gather
  246.6 5.1 %collective-permute-start.4 = (f32[66,16,1]{0,1,2:T(8,128)S(1)}, f32[66,16,1]{0,1,2:T(8,128)S(1)}, u32[]{:S(2)}, u32[]{:S(2)}) collective-permute-start(f32[66,16,1]{0,1,2:T(8,128)S(1)} %copy.73), channel_id=1, source_target_pairs={{0,16},{4,20},{8,24},{12,28},{16,0},{20,4},{24,8},{28,12},{1,17},{... | collective-permute-start | bytes 12680 | tf_op jit(solution)/shard_map/ppermute | solution.py:38
  258.9 13.6 %multiply_add_fusion.5 = f32[64,16,1024]{2,1,0:T(8,128)S(1)} fusion(f32[66,16,1]{2,1,0:T(8,128)S(1)} %get-tuple-element.31, f32[1,16,1024]{2,1,0:T(8,128)S(1)} %collective-permute-done.3, f32[64,16,896]{2,1,0:T(8,128)} %copy-done, f32[64,16,128]{2,1,0:T(8,128)S(1)} %slice_add_fusion, f32[1,16,1024]{2,1,0:T(8,128)S(1)} %collective-permute-done.2, ...), kind=kLoop, calls=%fused_computation.90 | loop fusion | flops 39845888 | bytes 8528128 | tf_op jit(solution)/shard_map/add | solution.py:52
  278.9 6.0 %collective-permute-start.9 = (f32[66,16,1]{0,1,2:T(8,128)S(1)}, f32[66,16,1]{0,1,2:T(8,128)S(1)}, u32[]{:S(2)}, u32[]{:S(2)}) collective-permute-start(f32[66,16,1]{0,1,2:T(8,128)S(1)} %copy.79), channel_id=1, source_target_pairs={{0,16},{4,20},{8,24},{12,28},{16,0},{20,4},{24,8},{28,12},{1,17},{... | collective-permute-start | bytes 12680 | tf_op jit(solution)/shard_map/ppermute | solution.py:38
  286.8 4.5 %collective-permute-start.10 = (f32[66,16,1]{0,1,2:T(8,128)S(1)}, f32[66,16,1]{0,1,2:T(8,128)S(1)}, u32[]{:S(2)}, u32[]{:S(2)}) collective-permute-start(f32[66,16,1]{0,1,2:T(8,128)S(1)} %copy.80), channel_id=1, source_target_pairs={{0,1},{1,2},{2,3},{4,5},{5,6},{6,7},{8,9},{9,10},{10,11},{12,13},{... | collective-permute-start | bytes 12680 | tf_op jit(solution)/shard_map/ppermute | solution.py:28
  292.5 12.5 %multiply_add_fusion.4 = f32[64,16,1024]{2,1,0:T(8,128)S(1)} fusion(f32[64,16,1024]{2,1,0:T(8,128)} %copy-done.2, f32[66,16,1]{2,1,0:T(8,128)S(1)} %get-tuple-element.29, f32[1,16,1024]{2,1,0:T(8,128)S(1)} %collective-permute-done.8, f32[1,16,1024]{2,1,0:T(8,128)S(1)} %collective-permute-done.7, f32[66,16,1]{2,1,0:T(8,128)S(1)} %broadcast_select_fusion.11), kind=kLoop, calls=%fused_computation.89 | loop fusion | flops 34603008 | bytes 8528128 | tf_op jit(solution)/shard_map/add | solution.py:52
  311.2 6.9 %collective-permute-start.14 = (f32[66,16,1]{0,1,2:T(8,128)S(1)}, f32[66,16,1]{0,1,2:T(8,128)S(1)}, u32[]{:S(2)}, u32[]{:S(2)}) collective-permute-start(f32[66,16,1]{0,1,2:T(8,128)S(1)} %copy.85), channel_id=1, source_target_pairs={{0,16},{4,20},{8,24},{12,28},{16,0},{20,4},{24,8},{28,12},{1,17},{... | collective-permute-start | bytes 12680 | tf_op jit(solution)/shard_map/ppermute | solution.py:38
  325.7 12.5 %multiply_add_fusion.3 = f32[64,16,1024]{2,1,0:T(8,128)S(1)} fusion(f32[64,16,1024]{2,1,0:T(8,128)} %copy-done.3, f32[66,16,1]{2,1,0:T(8,128)S(1)} %get-tuple-element.27, f32[1,16,1024]{2,1,0:T(8,128)S(1)} %collective-permute-done.13, f32[1,16,1024]{2,1,0:T(8,128)S(1)} %collective-permute-done.12, f32[66,16,1]{2,1,0:T(8,128)S(1)} %broadcast_select_fusion.10), kind=kLoop, calls=%fused_computation.88 | loop fusion | flops 34603008 | bytes 8528128 | tf_op jit(solution)/shard_map/add | solution.py:52
  343.9 6.9 %collective-permute-start.19 = (f32[66,16,1]{0,1,2:T(8,128)S(1)}, f32[66,16,1]{0,1,2:T(8,128)S(1)}, u32[]{:S(2)}, u32[]{:S(2)}) collective-permute-start(f32[66,16,1]{0,1,2:T(8,128)S(1)} %copy.91), channel_id=1, source_target_pairs={{0,16},{4,20},{8,24},{12,28},{16,0},{20,4},{24,8},{28,12},{1,17},{... | collective-permute-start | bytes 12680 | tf_op jit(solution)/shard_map/ppermute | solution.py:38
  352.7 4.7 %collective-permute-start.20 = (f32[66,16,1]{0,1,2:T(8,128)S(1)}, f32[66,16,1]{0,1,2:T(8,128)S(1)}, u32[]{:S(2)}, u32[]{:S(2)}) collective-permute-start(f32[66,16,1]{0,1,2:T(8,128)S(1)} %copy.92), channel_id=1, source_target_pairs={{0,1},{1,2},{2,3},{4,5},{5,6},{6,7},{8,9},{9,10},{10,11},{12,13},{... | collective-permute-start | bytes 12680 | tf_op jit(solution)/shard_map/ppermute | solution.py:28
  358.5 12.5 %multiply_add_fusion.2 = f32[64,16,1024]{2,1,0:T(8,128)S(1)} fusion(f32[64,16,1024]{2,1,0:T(8,128)} %copy-done.4, f32[66,16,1]{2,1,0:T(8,128)S(1)} %get-tuple-element.25, f32[1,16,1024]{2,1,0:T(8,128)S(1)} %collective-permute-done.18, f32[1,16,1024]{2,1,0:T(8,128)S(1)} %collective-permute-done.17, f32[66,16,1]{2,1,0:T(8,128)S(1)} %broadcast_select_fusion.9), kind=kLoop, calls=%fused_computation.87 | loop fusion | flops 34603008 | bytes 8528128 | tf_op jit(solution)/shard_map/add | solution.py:52
  376.6 6.9 %collective-permute-start.24 = (f32[66,16,1]{0,1,2:T(8,128)S(1)}, f32[66,16,1]{0,1,2:T(8,128)S(1)}, u32[]{:S(2)}, u32[]{:S(2)}) collective-permute-start(f32[66,16,1]{0,1,2:T(8,128)S(1)} %copy.97), channel_id=1, source_target_pairs={{0,16},{4,20},{8,24},{12,28},{16,0},{20,4},{24,8},{28,12},{1,17},{... | collective-permute-start | bytes 12680 | tf_op jit(solution)/shard_map/ppermute | solution.py:38
  391.2 12.5 %multiply_add_fusion.1 = f32[64,16,1024]{2,1,0:T(8,128)S(1)} fusion(f32[64,16,1024]{2,1,0:T(8,128)} %copy-done.5, f32[66,16,1]{2,1,0:T(8,128)S(1)} %get-tuple-element.23, f32[1,16,1024]{2,1,0:T(8,128)S(1)} %collective-permute-done.23, f32[1,16,1024]{2,1,0:T(8,128)S(1)} %collective-permute-done.22, f32[66,16,1]{2,1,0:T(8,128)S(1)} %broadcast_select_fusion.8), kind=kLoop, calls=%fused_computation.86 | loop fusion | flops 34603008 | bytes 8528128 | tf_op jit(solution)/shard_map/add | solution.py:52
  409.4 6.9 %collective-permute-start.29 = (f32[66,16,1]{0,1,2:T(8,128)S(1)}, f32[66,16,1]{0,1,2:T(8,128)S(1)}, u32[]{:S(2)}, u32[]{:S(2)}) collective-permute-start(f32[66,16,1]{0,1,2:T(8,128)S(1)} %copy.103), channel_id=1, source_target_pairs={{0,16},{4,20},{8,24},{12,28},{16,0},{20,4},{24,8},{28,12},{1,17},{... | collective-permute-start | bytes 12680 | tf_op jit(solution)/shard_map/ppermute | solution.py:38
  423.9 15.6 %multiply_add_fusion = f32[64,16,1024]{2,1,0:T(8,128)} fusion(f32[64,16,1024]{2,1,0:T(8,128)} %copy-done.1, f32[66,16,1]{2,1,0:T(8,128)S(1)} %get-tuple-element.21, f32[1,16,1024]{2,1,0:T(8,128)S(1)} %collective-permute-done.28, f32[1,16,1024]{2,1,0:T(8,128)S(1)} %collective-permute-done.27, f32[66,16,1]{2,1,0:T(8,128)S(1)} %broadcast_select_fusion.7), kind=kLoop, calls=%fused_computation.85 | loop fusion | flops 34603008 | bytes 8528128 | tf_op jit(solution)/shard_map/add | solution.py:52
  (217 shorter events, 153.7 us)
Async XLA Ops:
  2.8 70.3 %collective-permute-start.1 = (f32[64,16,384]{2,1,0:T(8,128)}, f32[64,16,384]{2,1,0:T(8,128)S(1)}, u32[]{:S(2)}, u32[]{:S(2)}) collective-permute-start(f32[64,16,384]{2,1,0:T(8,128)} %slice.193), channel_id=1, source_target_pairs={{0,16},{4,20},{8,24},{12,28},{16,0},{20,4},{24,8},{28,12},{1,17},{... | collective-permute-start | bytes 4718600 | tf_op jit(solution)/shard_map/ppermute | solution.py:38
  5.1 77.3 %collective-permute-start = (f32[64,16,384]{2,1,0:T(8,128)}, f32[64,16,384]{2,1,0:T(8,128)}, u32[]{:S(2)}, u32[]{:S(2)}) collective-permute-start(f32[64,16,384]{2,1,0:T(8,128)} %slice.193), channel_id=1, source_target_pairs={{1,0},{2,1},{3,2},{5,4},{6,5},{7,6},{9,8},{10,9},{11,10},{13,12},{... | collective-permute-start | bytes 4718600 | tf_op jit(solution)/shard_map/ppermute | solution.py:18
  241.2 1.4 collective-permute-start.2
  241.2 3.8 collective-permute-start.3
  245.3 6.4 %collective-permute-start.6 = (f32[66,16,1]{0,1,2:T(8,128)S(1)}, f32[66,16,1]{0,1,2:T(8,128)S(1)}, u32[]{:S(2)}, u32[]{:S(2)}) collective-permute-start(f32[66,16,1]{0,1,2:T(8,128)S(1)} %copy.73), channel_id=1, source_target_pairs={{1,0},{2,1},{3,2},{5,4},{6,5},{7,6},{9,8},{10,9},{11,10},{13,12},{... | collective-permute-start | bytes 12680 | tf_op jit(solution)/shard_map/ppermute | solution.py:31
  246.6 11.2 %collective-permute-start.4 = (f32[66,16,1]{0,1,2:T(8,128)S(1)}, f32[66,16,1]{0,1,2:T(8,128)S(1)}, u32[]{:S(2)}, u32[]{:S(2)}) collective-permute-start(f32[66,16,1]{0,1,2:T(8,128)S(1)} %copy.73), channel_id=1, source_target_pairs={{0,16},{4,20},{8,24},{12,28},{16,0},{20,4},{24,8},{28,12},{1,17},{... | collective-permute-start | bytes 12680 | tf_op jit(solution)/shard_map/ppermute | solution.py:38
  253.7 4.8 %collective-permute-start.5 = (f32[66,16,1]{0,1,2:T(8,128)S(1)}, f32[66,16,1]{0,1,2:T(8,128)S(1)}, u32[]{:S(2)}, u32[]{:S(2)}) collective-permute-start(f32[66,16,1]{0,1,2:T(8,128)S(1)} %copy.74), channel_id=1, source_target_pairs={{0,1},{1,2},{2,3},{4,5},{5,6},{6,7},{8,9},{9,10},{10,11},{12,13},{... | collective-permute-start | bytes 12680 | tf_op jit(solution)/shard_map/ppermute | solution.py:28
  272.5 2.4 collective-permute-start.7
  273.5 3.7 collective-permute-start.8
  277.6 7.3 %collective-permute-start.11 = (f32[66,16,1]{0,1,2:T(8,128)S(1)}, f32[66,16,1]{0,1,2:T(8,128)S(1)}, u32[]{:S(2)}, u32[]{:S(2)}) collective-permute-start(f32[66,16,1]{0,1,2:T(8,128)S(1)} %copy.79), channel_id=1, source_target_pairs={{1,0},{2,1},{3,2},{5,4},{6,5},{7,6},{9,8},{10,9},{11,10},{13,12},{... | collective-permute-start | bytes 12680 | tf_op jit(solution)/shard_map/ppermute | solution.py:31
  278.9 12.4 %collective-permute-start.9 = (f32[66,16,1]{0,1,2:T(8,128)S(1)}, f32[66,16,1]{0,1,2:T(8,128)S(1)}, u32[]{:S(2)}, u32[]{:S(2)}) collective-permute-start(f32[66,16,1]{0,1,2:T(8,128)S(1)} %copy.79), channel_id=1, source_target_pairs={{0,16},{4,20},{8,24},{12,28},{16,0},{20,4},{24,8},{28,12},{1,17},{... | collective-permute-start | bytes 12680 | tf_op jit(solution)/shard_map/ppermute | solution.py:38
  286.8 5.3 %collective-permute-start.10 = (f32[66,16,1]{0,1,2:T(8,128)S(1)}, f32[66,16,1]{0,1,2:T(8,128)S(1)}, u32[]{:S(2)}, u32[]{:S(2)}) collective-permute-start(f32[66,16,1]{0,1,2:T(8,128)S(1)} %copy.80), channel_id=1, source_target_pairs={{0,1},{1,2},{2,3},{4,5},{5,6},{6,7},{8,9},{9,10},{10,11},{12,13},{... | collective-permute-start | bytes 12680 | tf_op jit(solution)/shard_map/ppermute | solution.py:28
  305.0 2.1 collective-permute-start.12
  305.8 3.7 collective-permute-start.13
  309.9 8.2 %collective-permute-start.16 = (f32[66,16,1]{0,1,2:T(8,128)S(1)}, f32[66,16,1]{0,1,2:T(8,128)S(1)}, u32[]{:S(2)}, u32[]{:S(2)}) collective-permute-start(f32[66,16,1]{0,1,2:T(8,128)S(1)} %copy.85), channel_id=1, source_target_pairs={{1,0},{2,1},{3,2},{5,4},{6,5},{7,6},{9,8},{10,9},{11,10},{13,12},{... | collective-permute-start | bytes 12680 | tf_op jit(solution)/shard_map/ppermute | solution.py:31
  311.2 13.4 %collective-permute-start.14 = (f32[66,16,1]{0,1,2:T(8,128)S(1)}, f32[66,16,1]{0,1,2:T(8,128)S(1)}, u32[]{:S(2)}, u32[]{:S(2)}) collective-permute-start(f32[66,16,1]{0,1,2:T(8,128)S(1)} %copy.85), channel_id=1, source_target_pairs={{0,16},{4,20},{8,24},{12,28},{16,0},{20,4},{24,8},{28,12},{1,17},{... | collective-permute-start | bytes 12680 | tf_op jit(solution)/shard_map/ppermute | solution.py:38
  320.0 5.3 %collective-permute-start.15 = (f32[66,16,1]{0,1,2:T(8,128)S(1)}, f32[66,16,1]{0,1,2:T(8,128)S(1)}, u32[]{:S(2)}, u32[]{:S(2)}) collective-permute-start(f32[66,16,1]{0,1,2:T(8,128)S(1)} %copy.86), channel_id=1, source_target_pairs={{0,1},{1,2},{2,3},{4,5},{5,6},{6,7},{8,9},{9,10},{10,11},{12,13},{... | collective-permute-start | bytes 12680 | tf_op jit(solution)/shard_map/ppermute | solution.py:28
  338.3 1.6 collective-permute-start.17
  338.6 3.7 collective-permute-start.18
  342.6 8.2 %collective-permute-start.21 = (f32[66,16,1]{0,1,2:T(8,128)S(1)}, f32[66,16,1]{0,1,2:T(8,128)S(1)}, u32[]{:S(2)}, u32[]{:S(2)}) collective-permute-start(f32[66,16,1]{0,1,2:T(8,128)S(1)} %copy.91), channel_id=1, source_target_pairs={{1,0},{2,1},{3,2},{5,4},{6,5},{7,6},{9,8},{10,9},{11,10},{13,12},{... | collective-permute-start | bytes 12680 | tf_op jit(solution)/shard_map/ppermute | solution.py:31
  343.9 13.6 %collective-permute-start.19 = (f32[66,16,1]{0,1,2:T(8,128)S(1)}, f32[66,16,1]{0,1,2:T(8,128)S(1)}, u32[]{:S(2)}, u32[]{:S(2)}) collective-permute-start(f32[66,16,1]{0,1,2:T(8,128)S(1)} %copy.91), channel_id=1, source_target_pairs={{0,16},{4,20},{8,24},{12,28},{16,0},{20,4},{24,8},{28,12},{1,17},{... | collective-permute-start | bytes 12680 | tf_op jit(solution)/shard_map/ppermute | solution.py:38
  352.7 5.3 %collective-permute-start.20 = (f32[66,16,1]{0,1,2:T(8,128)S(1)}, f32[66,16,1]{0,1,2:T(8,128)S(1)}, u32[]{:S(2)}, u32[]{:S(2)}) collective-permute-start(f32[66,16,1]{0,1,2:T(8,128)S(1)} %copy.92), channel_id=1, source_target_pairs={{0,1},{1,2},{2,3},{4,5},{5,6},{6,7},{8,9},{9,10},{10,11},{12,13},{... | collective-permute-start | bytes 12680 | tf_op jit(solution)/shard_map/ppermute | solution.py:28
  371.0 1.6 collective-permute-start.22
  371.3 3.7 collective-permute-start.23
  375.3 8.2 %collective-permute-start.26 = (f32[66,16,1]{0,1,2:T(8,128)S(1)}, f32[66,16,1]{0,1,2:T(8,128)S(1)}, u32[]{:S(2)}, u32[]{:S(2)}) collective-permute-start(f32[66,16,1]{0,1,2:T(8,128)S(1)} %copy.97), channel_id=1, source_target_pairs={{1,0},{2,1},{3,2},{5,4},{6,5},{7,6},{9,8},{10,9},{11,10},{13,12},{... | collective-permute-start | bytes 12680 | tf_op jit(solution)/shard_map/ppermute | solution.py:31
  376.6 13.4 %collective-permute-start.24 = (f32[66,16,1]{0,1,2:T(8,128)S(1)}, f32[66,16,1]{0,1,2:T(8,128)S(1)}, u32[]{:S(2)}, u32[]{:S(2)}) collective-permute-start(f32[66,16,1]{0,1,2:T(8,128)S(1)} %copy.97), channel_id=1, source_target_pairs={{0,16},{4,20},{8,24},{12,28},{16,0},{20,4},{24,8},{28,12},{1,17},{... | collective-permute-start | bytes 12680 | tf_op jit(solution)/shard_map/ppermute | solution.py:38
  385.5 5.3 %collective-permute-start.25 = (f32[66,16,1]{0,1,2:T(8,128)S(1)}, f32[66,16,1]{0,1,2:T(8,128)S(1)}, u32[]{:S(2)}, u32[]{:S(2)}) collective-permute-start(f32[66,16,1]{0,1,2:T(8,128)S(1)} %copy.98), channel_id=1, source_target_pairs={{0,1},{1,2},{2,3},{4,5},{5,6},{6,7},{8,9},{9,10},{10,11},{12,13},{... | collective-permute-start | bytes 12680 | tf_op jit(solution)/shard_map/ppermute | solution.py:28
  403.7 1.6 collective-permute-start.27
  404.0 3.7 collective-permute-start.28
  408.1 8.2 %collective-permute-start.31 = (f32[66,16,1]{0,1,2:T(8,128)S(1)}, f32[66,16,1]{0,1,2:T(8,128)S(1)}, u32[]{:S(2)}, u32[]{:S(2)}) collective-permute-start(f32[66,16,1]{0,1,2:T(8,128)S(1)} %copy.103), channel_id=1, source_target_pairs={{1,0},{2,1},{3,2},{5,4},{6,5},{7,6},{9,8},{10,9},{11,10},{13,12},{... | collective-permute-start | bytes 12680 | tf_op jit(solution)/shard_map/ppermute | solution.py:31
  409.4 13.4 %collective-permute-start.29 = (f32[66,16,1]{0,1,2:T(8,128)S(1)}, f32[66,16,1]{0,1,2:T(8,128)S(1)}, u32[]{:S(2)}, u32[]{:S(2)}) collective-permute-start(f32[66,16,1]{0,1,2:T(8,128)S(1)} %copy.103), channel_id=1, source_target_pairs={{0,16},{4,20},{8,24},{12,28},{16,0},{20,4},{24,8},{28,12},{1,17},{... | collective-permute-start | bytes 12680 | tf_op jit(solution)/shard_map/ppermute | solution.py:38
  418.2 5.3 %collective-permute-start.30 = (f32[66,16,1]{0,1,2:T(8,128)S(1)}, f32[66,16,1]{0,1,2:T(8,128)S(1)}, u32[]{:S(2)}, u32[]{:S(2)}) collective-permute-start(f32[66,16,1]{0,1,2:T(8,128)S(1)} %copy.104), channel_id=1, source_target_pairs={{0,1},{1,2},{2,3},{4,5},{5,6},{6,7},{8,9},{9,10},{10,11},{12,13},{... | collective-permute-start | bytes 12680 | tf_op jit(solution)/shard_map/ppermute | solution.py:28
  (10 other events, 45.6 us)
where the time goes:
time: 447 us; the launch traced here: 440 us
  local copies, waits for them, and re-layouts  179 us (40%)
  other arithmetic  95.4 us (21%)
  waiting for transfers between devices  83.3 us (19%)
  starting transfers between devices  81.3 us (18%)
    gather x80, local copies, waits for them, and re-layouts  149 us
    add x6, other arithmetic, diffuse_once(): return centre_cells + time_step * summed  79.2 us
    ppermute x7, waiting for transfers between devices, shifted_2(): return lax.ppermute(x, axis, [(i, (i + by) % size) for i in range(size)])  60.3 us
    ppermute x7, starting transfers between devices, shifted_2(): return lax.ppermute(x, axis, [(i, (i + by) % size) for i in range(size)])  41.1 us
    ppermute x12, starting transfers between devices, padded_2(): lax.ppermute(lax.slice_in_dim(block, block.shape[dim] - width, None, axis...  29.8 us
    ppermute x12, waiting for transfers between devices, padded_2(): lax.ppermute(lax.slice_in_dim(block, 0, width, axis=dim), axis, backward)  14.3 us
    ppermute x12, starting transfers between devices, padded_2(): lax.ppermute(lax.slice_in_dim(block, 0, width, axis=dim), axis, backward)  9.06 us
  transfers between devices with their start and end apart: 32, of which 19 were waited for; matrix products, arithmetic and copies ran while one was open for 7% of the time, Pallas kernels for 0%

commit v1 on v0

v1 whole, which is shorter than its diff:
```python
import functools

import jax
import jax.numpy as jnp
from jax import lax
from jax.experimental import pallas as pl
from jax.experimental.pallas import tpu as pltpu
from jax.sharding import PartitionSpec as P

BAND = 384
STEPS = 6
LANES = 128
BAND_BLOCKS = BAND // LANES
TIME_STEP = 0.2
EDGE_SCALE = 0.8
SCALE = (1.0 / TIME_STEP) ** 0.5 / EDGE_SCALE
MESH = pl.DeviceIdType.MESH
VMEM_LIMIT = 56 * 1024 * 1024


def take_lanes(block, index):
    return jnp.take_along_axis(block, index, axis=1)


def align_kernel(margin_ref, data_ref, row_ref, band_ref, rim_ref):
    views, rows, width = data_ref.shape
    count = width // LANES
    is_last = lax.axis_index("col") == lax.axis_size("col") - 1
    lane = lax.broadcasted_iota(jnp.int32, (8, LANES), 1)
    sublane = lax.broadcasted_iota(jnp.int32, (8, LANES), 0)
    limit = jnp.where(is_last, width, 2 * width)

    def one_view(v, _):
        rim = jnp.zeros((8, LANES), jnp.float32)
        for h in range(rows // 8):
            rs = pl.ds(8 * h, 8)
            margin = margin_ref[rs, :]
            turn = (lane + margin) & (LANES - 1)
            stay = lane + (margin & (LANES - 1)) < LANES
            blocks_on = margin >> 7
            raw = [data_ref[v, rs, pl.ds(LANES * k, LANES)] for k in range(count)]
            turned = [take_lanes(b, turn) for b in raw]
            joined = [jnp.where(stay, turned[k], turned[(k + 1) % count]) for k in range(count)]
            rolled = [
                jnp.where(
                    blocks_on == 1,
                    joined[(k + 1) % count],
                    jnp.where(blocks_on == 2, joined[(k + 2) % count], joined[(k + 3) % count]),
                )
                for k in range(count)
            ]
            edge = take_lanes(raw[-1], jnp.full((8, LANES), LANES - 1, jnp.int32))
            for k in range(count):
                kept = rolled[k]
                if k >= count - BAND_BLOCKS:
                    band_ref[v, rs, pl.ds(LANES * (k - count + BAND_BLOCKS), LANES)] = kept
                    kept = jnp.where(lane + LANES * k + margin < limit, kept, edge)
                row_ref[v, rs, pl.ds(LANES * k, LANES)] = kept
            row_ref[v, rs, pl.ds(width, LANES)] = jnp.where(
                jnp.logical_and(is_last, lane < LANES // 2), edge, rolled[-1]
            )
            head = take_lanes(rolled[0], lane & 7)
            rim = rim + jnp.where((lane >> 3) == sublane + 8 * h, head, 0.0)
        rim_ref[v] = jnp.sum(rim, axis=0, keepdims=True)
        return 0

    lax.fori_loop(0, views, one_view, 0)


def exchange_kernel(
    row_ref, band_ref, rim_ref,
    low_ref, high_ref, next_ref, mirror_ref, right_ref, facing_ref,
    send_sem, recv_sem,
):
    views = row_ref.shape[0]
    ang, col = lax.axis_index("ang"), lax.axis_index("col")
    n_ang, n_col = lax.axis_size("ang"), lax.axis_size("col")
    half = n_ang // 2
    d = STEPS
    up, down = lax.rem(ang + 1, n_ang), lax.rem(ang + n_ang - 1, n_ang)
    across = lax.rem(ang + half, n_ang)
    across_up, across_down = lax.rem(ang + half + 1, n_ang), lax.rem(ang + half - 1, n_ang)
    prev = jnp.maximum(col - 1, 0)
    after = jnp.minimum(col + 1, n_col - 1)
    has_prev, has_next, at_axis = col > 0, col < n_col - 1, col == 0

    barrier = pltpu.get_barrier_semaphore()

    def greet(a, c):
        pl.semaphore_signal(barrier, inc=1, device_id=(a, c), device_id_type=MESH)

    greet(up, col)
    greet(down, col)

    @pl.when(has_prev)
    def _():
        for a in (ang, up, down):
            greet(a, prev)

    @pl.when(has_next)
    def _():
        for a in (ang, up, down):
            greet(a, after)

    @pl.when(at_axis)
    def _():
        for a in (across, across_up, across_down):
            greet(a, col)

    peers = 2
    for present in (has_prev, has_next, at_axis):
        peers = peers + 3 * present.astype(jnp.int32)
    pl.semaphore_wait(barrier, peers)

    used = [0]

    def copy(src, dst, a, c):
        i = used[0]
        used[0] += 1
        return pltpu.make_async_remote_copy(
            src_ref=src, dst_ref=dst, send_sem=send_sem.at[i], recv_sem=recv_sem.at[i],
            device_id=(a, c), device_id_type=MESH,
        )

    first, last, whole = pl.ds(0, d), pl.ds(views - d, d), pl.ds(0, views)
    low_end, high_end, middle = pl.ds(0, d), pl.ds(views + d, d), pl.ds(d, views)
    tail = pl.ds(BAND - LANES, LANES)

    band_edges = [
        copy(band_ref.at[first], next_ref.at[pl.ds(d, d)], ang, prev),
        copy(band_ref.at[last], next_ref.at[pl.ds(views, d)], ang, prev),
    ]
    inner = views - 2 * d
    band_inner = [copy(band_ref.at[pl.ds(d, inner)], next_ref.at[pl.ds(2 * d, inner)], ang, prev)]
    rims = [
        copy(rim_ref.at[whole], right_ref.at[middle], ang, prev),
        copy(rim_ref.at[first], right_ref.at[high_end], down, prev),
        copy(rim_ref.at[last], right_ref.at[low_end], up, prev),
    ]
    mirrors = [
        copy(rim_ref.at[whole], facing_ref.at[middle], across, col),
        copy(rim_ref.at[first], facing_ref.at[high_end], across_down, col),
        copy(rim_ref.at[last], facing_ref.at[low_end], across_up, col),
        copy(band_ref.at[first, :, tail], mirror_ref.at[high_end], across_down, col),
        copy(band_ref.at[last, :, tail], mirror_ref.at[low_end], across_up, col),
        copy(band_ref.at[whole, :, tail], mirror_ref.at[middle], across, col),
    ]
    turns = [
        copy(row_ref.at[first], high_ref, down, col),
        copy(row_ref.at[last], low_ref, up, col),
    ]
    passed_on = [
        copy(next_ref.at[pl.ds(d, d)], next_ref.at[high_end], down, col),
        copy(next_ref.at[pl.ds(views, d)], next_ref.at[low_end], up, col),
    ]
    leftward = band_edges + rims + band_inner

    @pl.when(has_prev)
    def _():
        for c in leftward:
            c.start()

    @pl.when(at_axis)
    def _():
        for c in mirrors:
            c.start()

    for c in turns:
        c.start()

    @pl.when(has_next)
    def _():
        for c in band_edges:
            c.wait_recv()
        for c in passed_on:
            c.start()
        for c in rims + band_inner:
            c.wait_recv()
        for c in passed_on:
            c.wait()

    @pl.when(at_axis)
    def _():
        for c in mirrors:
            c.wait()

    for c in turns:
        c.wait()

    @pl.when(has_prev)
    def _():
        for c in leftward:
            c.wait_send()


def flux(delta):
    return delta * pl.reciprocal(5.0 + delta * delta, approx=True)


def diffuse_kernel(
    margin_ref, ramp_ref, row_ref, low_ref, high_ref, next_ref, mirror_ref, right_ref, facing_ref,
    out_ref, field,
):
    views, rows, reach = row_ref.shape
    width = reach - LANES
    count = width // LANES
    d = STEPS
    is_last = lax.axis_index("col") == lax.axis_size("col") - 1
    is_first = lax.axis_index("col") == 0
    lane = lax.broadcasted_iota(jnp.int32, (8, LANES), 1)
    sublane = lax.broadcasted_iota(jnp.int32, (8, LANES), 0)
    limit = jnp.where(is_last, 4 * width, width)

    def weight_of(position, spread):
        return jnp.clip(0.5 + (position.astype(jnp.float32) + 0.5) / spread, 0.0, 1.0)

    def stitch(source_ref, offset, length, h):
        rs = pl.ds(8 * h, 8)
        margin = margin_ref[rs, :]
        spread = 2.0 * ramp_ref[rs, :].astype(jnp.float32)
        head = weight_of(lane, spread)
        inner = weight_of(lane - LANES, spread)
        cell = (sublane + 8 * h) * 8

        def one(i, _):
            p = i + offset
            for k in range(1, count):
                block = source_ref[i, rs, pl.ds(LANES * k, LANES)]
                j = k - count + BAND_BLOCKS
                if j >= 0:
                    following = next_ref[p, rs, pl.ds(LANES * j, LANES)]
                    block = jnp.where(lane + LANES * k + margin < limit, block, following)
                field[p, rs, pl.ds(LANES * k, LANES)] = SCALE * block
            block = source_ref[i, rs, pl.ds(0, LANES)]
            facing = take_lanes(mirror_ref[p, rs, :], LANES - 1 - lane)
            blended = head * block + (1.0 - head) * facing
            field[p, rs, pl.ds(0, LANES)] = SCALE * jnp.where(is_first, blended, block)
            block = source_ref[i, rs, pl.ds(width, LANES)]
            facing = take_lanes(jnp.broadcast_to(facing_ref[p], (8, LANES)), cell + ((LANES - 1 - lane) & 7))
            blended = inner * block + (1.0 - inner) * facing
            inward = jnp.where(is_first, blended, block)
            outward = take_lanes(jnp.broadcast_to(right_ref[p], (8, LANES)), cell + (lane & 7))
            outward = jnp.where(is_last, block, outward)
            field[p, rs, pl.ds(width, LANES)] = SCALE * jnp.where(lane < LANES // 2, outward, inward)
            return 0

        lax.fori_loop(0, length, one, 0)

    for h in range(rows // 8):
        stitch(low_ref, 0, d, h)
        stitch(row_ref, d, views, h)
        stitch(high_ref, views + d, d, h)

    for step in range(1, STEPS + 1):
        for h in range(rows // 8):
            rs = pl.ds(8 * h, 8)

            def one(v, carried):
                current, before = carried
                later = field[v + 1, rs, :]
                ahead = flux(later - current)
                outward = flux(pltpu.roll(current, reach - 1, 1) - current)
                inward = pltpu.roll(outward, 1, 1)
                updated = current + ((ahead - before) + (outward - inward))
                if step < STEPS:
                    field[v, rs, :] = updated
                else:
                    out_ref[v - d, rs, :] = updated[:, :width] * (1.0 / SCALE)
                return later, ahead

            current = field[step, rs, :]
            before = flux(current - field[step - 1, rs, :])
            lax.fori_loop(step, views + 2 * d - step, one, (current, before))


def per_device(projections, margin, ramp_length):
    views, rows, width = projections.shape
    margin = jnp.broadcast_to(margin[:, None], (rows, LANES))
    ramp = jnp.broadcast_to(ramp_length[:, None], (rows, LANES))
    tall = views + 2 * STEPS
    reach = width + LANES
    f32 = jnp.float32
    shape = jax.ShapeDtypeStruct
    vmem = pl.BlockSpec(memory_space=pltpu.VMEM)
    anywhere = pl.BlockSpec(memory_space=pl.ANY)
    row, band, rim = pl.pallas_call(
        align_kernel,
        out_shape=(
            shape((views, rows, reach), f32),
            shape((views, rows, BAND), f32),
            shape((views, 1, LANES), f32),
        ),
        in_specs=[vmem] * 2,
        out_specs=(vmem,) * 3,
        compiler_params=pltpu.CompilerParams(vmem_limit_bytes=VMEM_LIMIT),
    )(margin, projections)
    parts = pl.pallas_call(
        exchange_kernel,
        out_shape=(
            shape((STEPS, rows, reach), f32),
            shape((STEPS, rows, reach), f32),
            shape((tall, rows, BAND), f32),
            shape((tall, rows, LANES), f32),
            shape((tall, 1, LANES), f32),
            shape((tall, 1, LANES), f32),
        ),
        in_specs=[anywhere] * 3,
        out_specs=(anywhere,) * 6,
        scratch_shapes=[pltpu.SemaphoreType.DMA((16,)), pltpu.SemaphoreType.DMA((16,))],
        compiler_params=pltpu.CompilerParams(collective_id=0, has_side_effects=True),
    )(row, band, rim)
    return pl.pallas_call(
        diffuse_kernel,
        out_shape=shape((views, rows, width), f32),
        in_specs=[vmem] * 9,
        out_specs=vmem,
        scratch_shapes=[pltpu.VMEM((tall, rows, reach), f32)],
        compiler_params=pltpu.CompilerParams(vmem_limit_bytes=VMEM_LIMIT),
    )(margin, ramp, row, *parts)


def solution(mesh):
    in_specs = (P("ang", None, "col"), P(), P())
    out_specs = P("ang", None, "col")
    return jax.shard_map(
        per_device, mesh=mesh, in_specs=in_specs, out_specs=out_specs, check_vma=False
    )
```

time: 447 us -> 214 us (0.48); the launches traced: 440 us -> 213 us
  Pallas kernels: 0 us -> 211 us
  local copies, waits for them, and re-layouts: 179 us -> 2.63 us
  other arithmetic: 95.4 us -> 0 us
  waiting for transfers between devices: 83.3 us -> 0 us
  starting transfers between devices: 81.3 us -> 0 us
    pallas_call x0 -> x3, Pallas kernels: none -> 211 us  [the longest x1 150 us: per_device(): pl.pallas_call(diffuse_kernel, out_shape=shape((views, rows, width), f32)...]
    gather x82 -> x0, local copies, waits for them, and re-layouts: 154 us -> none
    ppermute x32 -> x0, waiting for transfers between devices: 83.3 us -> none  [the longest x7 60.3 us: shifted_2(): return lax.ppermute(x, axis, [(i, (i + by) % size) for i in range(size)])]
    ppermute x32 -> x0, starting transfers between devices: 81.3 us -> none  [the longest x7 41.1 us: shifted_2(): return lax.ppermute(x, axis, [(i, (i + by) % size) for i in range(size)])]
    add x9 -> x0, other arithmetic: 79.3 us -> none  [the longest x6 79.2 us: diffuse_once(): return centre_cells + time_step * summed]
    select_n x13 -> x0, other arithmetic: 9.71 us -> none  [the longest x6 7.51 us: diffuse_round(): outward = jnp.where(is_last, reflected, padded[:, :, -rim_depth:])]
    ppermute x19 -> x0, local copies, waits for them, and re-layouts: 8.56 us -> none  [the longest x7 4.44 us: shifted_2(): return lax.ppermute(x, axis, [(i, (i + by) % size) for i in range(size)])]
    slice x20 -> x0, local copies, waits for them, and re-layouts: 7.91 us -> none  [the longest x1 2.84 us: stitch_direct(): leading = data[:, :, :BAND_MAX]]
  transfers between devices with their start and end apart: 32 -> 0, of which waited for: 19 -> 0; matrix products, arithmetic and copies ran while one was open for 7% -> 0% of each run, Pallas kernels for 0% -> 0%
where the time goes in v1:
time: 214 us; the launch traced here: 213 us
  Pallas kernels  211 us (99%)
  local copies, waits for them, and re-layouts  2.63 us (1%)
    pallas_call x1, Pallas kernels, per_device(): pl.pallas_call(diffuse_kernel, out_shape=shape((views, rows, width), f32)...  150 us
    pallas_call x1, Pallas kernels, per_device(): pl.pallas_call(exchange_kernel, out_shape=(shape((STEPS, rows, reach), f3...  45.1 us
    pallas_call x1, Pallas kernels, per_device(): pl.pallas_call(align_kernel, out_shape=(shape((views, rows, reach), f32),...  15.6 us

profile of v1, /device:TPU:9, one launch (start us, length us, event | category | flops | bytes accessed | tf_op | source)
XLA Modules:
  0.0 213.4 jit_solution(11493178500682199737)
XLA Ops:
  0.0 1.3 broadcast_in_dim.4.margin_ref
  1.3 1.3 broadcast_in_dim.5.ramp_ref
  2.6 15.6 %shard_map.37 = (f32[64,16,1152]{2,1,0:T(8,128)}, f32[64,16,384]{2,1,0:T(8,128)}, f32[64,1,128]{2,1,0:T(1,128)}) custom-call(s32[16,128]{1,0:T(8,128)} %broadcast_in_dim.4.margin_ref, f32[64,16,1024]{2,1,0:T(8,128)} %data_ref.1), custom_call_target="tpu_custom_call" | custom-call | tf_op jit(solution)/shard_map/pallas_call | solution.py:286
  18.2 45.1 %shard_map.38 = (f32[6,16,1152]{2,1,0:T(8,128)}, f32[6,16,1152]{2,1,0:T(8,128)}, f32[76,16,384]{2,1,0:T(8,128)}, f32[76,16,128]{2,1,0:T(8,128)}, f32[76,1,128]{2,1,0:T(1,128)}, /*index=5*/f32[76,1,128]{2,1,0:T(1,128)}) custom-call(f32[64,16,1152]{2,1,0:T(8,128)} %get-tuple-element.14.row_ref, f32[64,16,384]{2,1,0:T(8,128)} %get-tuple-element.15.band_ref, ...), custom_call_target="tpu_custom_call" | custom-call | tf_op jit(solution)/shard_map/pallas_call | solution.py:297
  63.3 150.0 %shard_map.39 = f32[64,16,1024]{2,1,0:T(8,128)} custom-call(s32[16,128]{1,0:T(8,128)} %broadcast_in_dim.4.margin_ref, s32[16,128]{1,0:T(8,128)} %broadcast_in_dim.5.ramp_ref, f32[64,16,1152]{2,1,0:T(8,128)} %get-tuple-element.14.row_ref, f32[6,16,1152]{2,1,0:T(8,128)} %get-tuple-element.17.low_ref, f32[6,16,1152]{2,1,0:T(8,128)} %get-tuple-element.18.high_ref, ...), custom_call_target="tpu_custom_call" | custom-call | tf_op jit(solution)/shard_map/pallas_call | solution.py:312

commit v2 on v1

--- a/solution.py
+++ b/solution.py
@@ -16,6 +16,9 @@
 SCALE = (1.0 / TIME_STEP) ** 0.5 / EDGE_SCALE
 MESH = pl.DeviceIdType.MESH
 VMEM_LIMIT = 56 * 1024 * 1024
+VIEWS_AT_ONCE = 4
+ROWS_AT_ONCE = 16
+UNROLL = 4
 
 
 def take_lanes(block, index):
@@ -64,7 +67,7 @@
         rim_ref[v] = jnp.sum(rim, axis=0, keepdims=True)
         return 0
 
-    lax.fori_loop(0, views, one_view, 0)
+    lax.fori_loop(0, views, one_view, 0, unroll=UNROLL)
 
 
 def exchange_kernel(
@@ -244,33 +247,38 @@
             field[p, rs, pl.ds(width, LANES)] = SCALE * jnp.where(lane < LANES // 2, outward, inward)
             return 0
 
-        lax.fori_loop(0, length, one, 0)
+        lax.fori_loop(0, length, one, 0, unroll=2)
 
     for h in range(rows // 8):
         stitch(low_ref, 0, d, h)
         stitch(row_ref, d, views, h)
         stitch(high_ref, views + d, d, h)
 
+    slabs = range(0, rows, ROWS_AT_ONCE)
     for step in range(1, STEPS + 1):
-        for h in range(rows // 8):
-            rs = pl.ds(8 * h, 8)
-
-            def one(v, carried):
+        for first_row in slabs:
+            rs = pl.ds(first_row, ROWS_AT_ONCE)
+
+            def some(i, carried):
                 current, before = carried
-                later = field[v + 1, rs, :]
-                ahead = flux(later - current)
-                outward = flux(pltpu.roll(current, reach - 1, 1) - current)
-                inward = pltpu.roll(outward, 1, 1)
-                updated = current + ((ahead - before) + (outward - inward))
-                if step < STEPS:
-                    field[v, rs, :] = updated
-                else:
-                    out_ref[v - d, rs, :] = updated[:, :width] * (1.0 / SCALE)
-                return later, ahead
+                v = step + i * VIEWS_AT_ONCE
+                loaded = [field[v + 1 + u, rs, :] for u in range(VIEWS_AT_ONCE)]
+                for u, later in enumerate(loaded):
+                    ahead = flux(later - current)
+                    outward = flux(pltpu.roll(current, reach - 1, 1) - current)
+                    inward = pltpu.roll(outward, 1, 1)
+                    updated = current + ((ahead - before) + (outward - inward))
+                    if step < STEPS:
+                        field[v + u, rs, :] = updated
+                    else:
+                        out_ref[v + u - d, rs, :] = updated[:, :width] * (1.0 / SCALE)
+                    current, before = later, ahead
+                return current, before
 
             current = field[step, rs, :]
             before = flux(current - field[step - 1, rs, :])
-            lax.fori_loop(step, views + 2 * d - step, one, (current, before))
+            groups = pl.cdiv(views + 2 * (d - step), VIEWS_AT_ONCE)
+            lax.fori_loop(0, groups, some, (current, before))
 
 
 def per_device(projections, margin, ramp_length):
@@ -314,7 +322,7 @@
         out_shape=shape((views, rows, width), f32),
         in_specs=[vmem] * 9,
         out_specs=vmem,
-        scratch_shapes=[pltpu.VMEM((tall, rows, reach), f32)],
+        scratch_shapes=[pltpu.VMEM((tall + VIEWS_AT_ONCE + 1, rows, reach), f32)],
         compiler_params=pltpu.CompilerParams(vmem_limit_bytes=VMEM_LIMIT),
     )(margin, ramp, row, *parts)
 

time: 214 us -> 99.2 us (0.46)
  Pallas kernels: 211 us -> 96.4 us
    pallas_call x1, Pallas kernels: 150 us -> 42.3 us  [per_device(): pl.pallas_call(diffuse_kernel, out_shape=shape((views, rows, width), f32)...]
    pallas_call x1, Pallas kernels: 15.6 us -> 8.98 us  [per_device(): pl.pallas_call(align_kernel, out_shape=(shape((views, rows, reach), f32),...]
where the time goes in v2:
time: 99.2 us; the launch traced here: 99 us
  Pallas kernels  96.4 us (97%)
  local copies, waits for them, and re-layouts  2.63 us (3%)
    pallas_call x1, Pallas kernels, per_device(): pl.pallas_call(exchange_kernel, out_shape=(shape((STEPS, rows, reach), f3...  45.1 us
    pallas_call x1, Pallas kernels, per_device(): pl.pallas_call(diffuse_kernel, out_shape=shape((views, rows, width), f32)...  42.3 us
    pallas_call x1, Pallas kernels, per_device(): pl.pallas_call(align_kernel, out_shape=(shape((views, rows, reach), f32),...  8.98 us

profile of v2, /device:TPU:9, one launch (start us, length us, event | category | flops | bytes accessed | tf_op | source)
XLA Modules:
  0.0 99.0 jit_solution(13809274399338071030)
XLA Ops:
  0.0 1.3 %broadcast_in_dim.4.margin_ref = s32[16,128]{1,0:T(8,128)} broadcast(s32[16]{0:T(128)} %param.4), dimensions={0} | broadcast | bytes 8256 | tf_op jit(solution)/shard_map/broadcast_in_dim | solution.py:286
  1.3 1.3 %broadcast_in_dim.5.ramp_ref = s32[16,128]{1,0:T(8,128)} broadcast(s32[16]{0:T(128)} %param.5), dimensions={0} | broadcast | bytes 8256 | tf_op jit(solution)/shard_map/broadcast_in_dim | solution.py:287
  2.6 9.0 %shard_map.37 = (f32[64,16,1152]{2,1,0:T(8,128)}, f32[64,16,384]{2,1,0:T(8,128)}, f32[64,1,128]{2,1,0:T(1,128)}) custom-call(s32[16,128]{1,0:T(8,128)} %broadcast_in_dim.4.margin_ref, f32[64,16,1024]{2,1,0:T(8,128)} %data_ref.1), custom_call_target="tpu_custom_call" | custom-call | tf_op jit(solution)/shard_map/pallas_call | solution.py:294
  11.6 45.1 %shard_map.38 = (f32[6,16,1152]{2,1,0:T(8,128)}, f32[6,16,1152]{2,1,0:T(8,128)}, f32[76,16,384]{2,1,0:T(8,128)}, f32[76,16,128]{2,1,0:T(8,128)}, f32[76,1,128]{2,1,0:T(1,128)}, /*index=5*/f32[76,1,128]{2,1,0:T(1,128)}) custom-call(f32[64,16,1152]{2,1,0:T(8,128)} %get-tuple-element.14.row_ref, f32[64,16,384]{2,1,0:T(8,128)} %get-tuple-element.15.band_ref, ...), custom_call_target="tpu_custom_call" | custom-call | tf_op jit(solution)/shard_map/pallas_call | solution.py:305
  56.7 42.3 %shard_map.39 = f32[64,16,1024]{2,1,0:T(8,128)} custom-call(s32[16,128]{1,0:T(8,128)} %broadcast_in_dim.4.margin_ref, s32[16,128]{1,0:T(8,128)} %broadcast_in_dim.5.ramp_ref, f32[64,16,1152]{2,1,0:T(8,128)} %get-tuple-element.14.row_ref, f32[6,16,1152]{2,1,0:T(8,128)} %get-tuple-element.17.low_ref, f32[6,16,1152]{2,1,0:T(8,128)} %get-tuple-element.18.high_ref, ...), custom_call_target="tpu_custom_call" | custom-call | tf_op jit(solution)/shard_map/pallas_call | solution.py:320

commit v3 on v2

--- a/solution.py
+++ b/solution.py
@@ -247,7 +247,7 @@
             field[p, rs, pl.ds(width, LANES)] = SCALE * jnp.where(lane < LANES // 2, outward, inward)
             return 0
 
-        lax.fori_loop(0, length, one, 0, unroll=2)
+        lax.fori_loop(0, length, one, 0, unroll=8 if length % 8 == 0 else 6)
 
     for h in range(rows // 8):
         stitch(low_ref, 0, d, h)

time: 99.2 us -> 95.2 us (0.960)
  Pallas kernels: 96.4 us -> 92.3 us
    pallas_call x1, Pallas kernels: 42.3 us -> 38.2 us  [per_device(): pl.pallas_call(diffuse_kernel, out_shape=shape((views, rows, width), f32)...]
where the time goes in v3:
time: 95.2 us; the launch traced here: 95 us
  Pallas kernels  92.3 us (97%)
  local copies, waits for them, and re-layouts  2.63 us (3%)
    pallas_call x1, Pallas kernels, per_device(): pl.pallas_call(exchange_kernel, out_shape=(shape((STEPS, rows, reach), f3...  45.1 us
    pallas_call x1, Pallas kernels, per_device(): pl.pallas_call(diffuse_kernel, out_shape=shape((views, rows, width), f32)...  38.2 us
    pallas_call x1, Pallas kernels, per_device(): pl.pallas_call(align_kernel, out_shape=(shape((views, rows, reach), f32),...  8.98 us

profile of v3, /device:TPU:9, one launch (start us, length us, event | category | flops | bytes accessed | tf_op | source)
XLA Modules:
  0.0 95.0 jit_solution(8652913194094617348)
XLA Ops:
  0.0 1.3 %broadcast_in_dim.4.margin_ref = s32[16,128]{1,0:T(8,128)} broadcast(s32[16]{0:T(128)} %param.4), dimensions={0} | broadcast | bytes 8256 | tf_op jit(solution)/shard_map/broadcast_in_dim | solution.py:286
  1.3 1.3 %broadcast_in_dim.5.ramp_ref = s32[16,128]{1,0:T(8,128)} broadcast(s32[16]{0:T(128)} %param.5), dimensions={0} | broadcast | bytes 8256 | tf_op jit(solution)/shard_map/broadcast_in_dim | solution.py:287
  2.6 9.0 %shard_map.37 = (f32[64,16,1152]{2,1,0:T(8,128)}, f32[64,16,384]{2,1,0:T(8,128)}, f32[64,1,128]{2,1,0:T(1,128)}) custom-call(s32[16,128]{1,0:T(8,128)} %broadcast_in_dim.4.margin_ref, f32[64,16,1024]{2,1,0:T(8,128)} %data_ref.1), custom_call_target="tpu_custom_call" | custom-call | tf_op jit(solution)/shard_map/pallas_call | solution.py:294
  11.6 45.1 %shard_map.38 = (f32[6,16,1152]{2,1,0:T(8,128)}, f32[6,16,1152]{2,1,0:T(8,128)}, f32[76,16,384]{2,1,0:T(8,128)}, f32[76,16,128]{2,1,0:T(8,128)}, f32[76,1,128]{2,1,0:T(1,128)}, /*index=5*/f32[76,1,128]{2,1,0:T(1,128)}) custom-call(f32[64,16,1152]{2,1,0:T(8,128)} %get-tuple-element.14.row_ref, f32[64,16,384]{2,1,0:T(8,128)} %get-tuple-element.15.band_ref, ...), custom_call_target="tpu_custom_call" | custom-call | tf_op jit(solution)/shard_map/pallas_call | solution.py:305
  56.7 38.2 %shard_map.39 = f32[64,16,1024]{2,1,0:T(8,128)} custom-call(s32[16,128]{1,0:T(8,128)} %broadcast_in_dim.4.margin_ref, s32[16,128]{1,0:T(8,128)} %broadcast_in_dim.5.ramp_ref, f32[64,16,1152]{2,1,0:T(8,128)} %get-tuple-element.14.row_ref, f32[6,16,1152]{2,1,0:T(8,128)} %get-tuple-element.17.low_ref, f32[6,16,1152]{2,1,0:T(8,128)} %get-tuple-element.18.high_ref, ...), custom_call_target="tpu_custom_call" | custom-call | tf_op jit(solution)/shard_map/pallas_call | solution.py:320

commit v4 on v3

--- a/solution.py
+++ b/solution.py
@@ -37,7 +37,7 @@
         rim = jnp.zeros((8, LANES), jnp.float32)
         for h in range(rows // 8):
             rs = pl.ds(8 * h, 8)
-            margin = margin_ref[rs, :]
+            margin = jnp.broadcast_to(margin_ref[rs, :], (8, LANES))
             turn = (lane + margin) & (LANES - 1)
             stay = lane + (margin & (LANES - 1)) < LANES
             blocks_on = margin >> 7
@@ -219,8 +219,8 @@
 
     def stitch(source_ref, offset, length, h):
         rs = pl.ds(8 * h, 8)
-        margin = margin_ref[rs, :]
-        spread = 2.0 * ramp_ref[rs, :].astype(jnp.float32)
+        margin = jnp.broadcast_to(margin_ref[rs, :], (8, LANES))
+        spread = 2.0 * jnp.broadcast_to(ramp_ref[rs, :], (8, LANES)).astype(jnp.float32)
         head = weight_of(lane, spread)
         inner = weight_of(lane - LANES, spread)
         cell = (sublane + 8 * h) * 8
@@ -283,8 +283,8 @@
 
 def per_device(projections, margin, ramp_length):
     views, rows, width = projections.shape
-    margin = jnp.broadcast_to(margin[:, None], (rows, LANES))
-    ramp = jnp.broadcast_to(ramp_length[:, None], (rows, LANES))
+    margin = margin[:, None]
+    ramp = ramp_length[:, None]
     tall = views + 2 * STEPS
     reach = width + LANES
     f32 = jnp.float32

time: 95.2 us -> 96 us (level)
  no operation moved by 1% of the time
where the time goes in v4:
time: 96 us; the launch traced here: 95.8 us
  Pallas kernels  93.1 us (97%)
  local copies, waits for them, and re-layouts  2.65 us (3%)
    pallas_call x1, Pallas kernels, per_device(): pl.pallas_call(exchange_kernel, out_shape=(shape((STEPS, rows, reach), f3...  45.1 us
    pallas_call x1, Pallas kernels, per_device(): pl.pallas_call(diffuse_kernel, out_shape=shape((views, rows, width), f32)...  38.3 us
    pallas_call x1, Pallas kernels, per_device(): pl.pallas_call(align_kernel, out_shape=(shape((views, rows, reach), f32),...  9.77 us

profile of v4, /device:TPU:9, one launch (start us, length us, event | category | flops | bytes accessed | tf_op | source)
XLA Modules:
  0.0 95.8 jit_solution(8945736811795125833)
XLA Ops:
  0.0 1.3 %copy.5.margin_ref = s32[16,1]{1,0:T(8,128)} copy(s32[16,1]{0,1:T(1,128)} %bitcast.2) | data formatting | bytes 128 | tf_op jit(solution)/shard_map/broadcast_in_dim | solution.py:286
  1.3 1.3 %copy.6.ramp_ref = s32[16,1]{1,0:T(8,128)} copy(s32[16,1]{0,1:T(1,128)} %bitcast.3) | data formatting | bytes 128 | tf_op jit(solution)/shard_map/broadcast_in_dim | solution.py:287
  2.6 9.8 %shard_map.37 = (f32[64,16,1152]{2,1,0:T(8,128)}, f32[64,16,384]{2,1,0:T(8,128)}, f32[64,1,128]{2,1,0:T(1,128)}) custom-call(s32[16,1]{1,0:T(8,128)} %copy.5.margin_ref, f32[64,16,1024]{2,1,0:T(8,128)} %data_ref.1), custom_call_target="tpu_custom_call" | custom-call | tf_op jit(solution)/shard_map/pallas_call | solution.py:294
  12.4 45.1 %shard_map.38 = (f32[6,16,1152]{2,1,0:T(8,128)}, f32[6,16,1152]{2,1,0:T(8,128)}, f32[76,16,384]{2,1,0:T(8,128)}, f32[76,16,128]{2,1,0:T(8,128)}, f32[76,1,128]{2,1,0:T(1,128)}, /*index=5*/f32[76,1,128]{2,1,0:T(1,128)}) custom-call(f32[64,16,1152]{2,1,0:T(8,128)} %get-tuple-element.14.row_ref, f32[64,16,384]{2,1,0:T(8,128)} %get-tuple-element.15.band_ref, ...), custom_call_target="tpu_custom_call" | custom-call | tf_op jit(solution)/shard_map/pallas_call | solution.py:305
  57.5 38.3 %shard_map.39 = f32[64,16,1024]{2,1,0:T(8,128)} custom-call(s32[16,1]{1,0:T(8,128)} %copy.5.margin_ref, s32[16,1]{1,0:T(8,128)} %copy.6.ramp_ref, f32[64,16,1152]{2,1,0:T(8,128)} %get-tuple-element.14.row_ref, f32[6,16,1152]{2,1,0:T(8,128)} %get-tuple-element.17.low_ref, f32[6,16,1152]{2,1,0:T(8,128)} %get-tuple-element.18.high_ref, ...), custom_call_target="tpu_custom_call" | custom-call | tf_op jit(solution)/shard_map/pallas_call | solution.py:320

commit v5 on v3

--- a/solution.py
+++ b/solution.py
@@ -262,8 +262,8 @@
             def some(i, carried):
                 current, before = carried
                 v = step + i * VIEWS_AT_ONCE
-                loaded = [field[v + 1 + u, rs, :] for u in range(VIEWS_AT_ONCE)]
-                for u, later in enumerate(loaded):
+                for u in range(VIEWS_AT_ONCE):
+                    later = field[v + 1 + u, rs, :]
                     ahead = flux(later - current)
                     outward = flux(pltpu.roll(current, reach - 1, 1) - current)
                     inward = pltpu.roll(outward, 1, 1)
@@ -287,6 +287,7 @@
     ramp = jnp.broadcast_to(ramp_length[:, None], (rows, LANES))
     tall = views + 2 * STEPS
     reach = width + LANES
+    chunk = 32
     f32 = jnp.float32
     shape = jax.ShapeDtypeStruct
     vmem = pl.BlockSpec(memory_space=pltpu.VMEM)
@@ -298,8 +299,16 @@
             shape((views, rows, BAND), f32),
             shape((views, 1, LANES), f32),
         ),
-        in_specs=[vmem] * 2,
-        out_specs=(vmem,) * 3,
+        grid=(views // chunk,),
+        in_specs=[
+            pl.BlockSpec((rows, LANES), lambda i: (0, 0)),
+            pl.BlockSpec((chunk, rows, width), lambda i: (i, 0, 0)),
+        ],
+        out_specs=(
+            pl.BlockSpec((chunk, rows, reach), lambda i: (i, 0, 0)),
+            pl.BlockSpec((chunk, rows, BAND), lambda i: (i, 0, 0)),
+            pl.BlockSpec((chunk, 1, LANES), lambda i: (i, 0, 0)),
+        ),
         compiler_params=pltpu.CompilerParams(vmem_limit_bytes=VMEM_LIMIT),
     )(margin, projections)
     parts = pl.pallas_call(

time: 95.2 us -> 93.6 us (0.983)
  Pallas kernels: 92.3 us -> 90.8 us
    pallas_call x1, Pallas kernels: 8.98 us -> 7.42 us  [per_device(): pl.pallas_call(align_kernel, out_shape=(shape((views, rows, reach), f32),...]
where the time goes in v5:
time: 93.6 us; the launch traced here: 93.4 us
  Pallas kernels  90.8 us (97%)
  local copies, waits for them, and re-layouts  2.63 us (3%)
    pallas_call x1, Pallas kernels, per_device(): pl.pallas_call(exchange_kernel, out_shape=(shape((STEPS, rows, reach), f3...  45.1 us
    pallas_call x1, Pallas kernels, per_device(): pl.pallas_call(diffuse_kernel, out_shape=shape((views, rows, width), f32)...  38.2 us
    pallas_call x1, Pallas kernels, per_device(): pl.pallas_call(align_kernel, out_shape=(shape((views, rows, reach), f32),...  7.42 us

profile of v5, /device:TPU:9, one launch (start us, length us, event | category | flops | bytes accessed | tf_op | source)
XLA Modules:
  0.0 93.4 jit_solution(4370169163691328283)
XLA Ops:
  0.0 1.3 %broadcast_in_dim.4.margin_ref = s32[16,128]{1,0:T(8,128)} broadcast(s32[16]{0:T(128)} %param.4), dimensions={0} | broadcast | bytes 8256 | tf_op jit(solution)/shard_map/broadcast_in_dim | solution.py:286
  1.3 1.3 %broadcast_in_dim.5.ramp_ref = s32[16,128]{1,0:T(8,128)} broadcast(s32[16]{0:T(128)} %param.5), dimensions={0} | broadcast | bytes 8256 | tf_op jit(solution)/shard_map/broadcast_in_dim | solution.py:287
  2.6 7.4 %shard_map.37 = (f32[64,16,1152]{2,1,0:T(8,128)}, f32[64,16,384]{2,1,0:T(8,128)}, f32[64,1,128]{2,1,0:T(1,128)}) custom-call(s32[16,128]{1,0:T(8,128)} %broadcast_in_dim.4.margin_ref, f32[64,16,1024]{2,1,0:T(8,128)} %data_ref.1), custom_call_target="tpu_custom_call" | custom-call | tf_op jit(solution)/shard_map/pallas_call | solution.py:295
  10.1 45.1 %shard_map.38 = (f32[6,16,1152]{2,1,0:T(8,128)}, f32[6,16,1152]{2,1,0:T(8,128)}, f32[76,16,384]{2,1,0:T(8,128)}, f32[76,16,128]{2,1,0:T(8,128)}, f32[76,1,128]{2,1,0:T(1,128)}, /*index=5*/f32[76,1,128]{2,1,0:T(1,128)}) custom-call(f32[64,16,1152]{2,1,0:T(8,128)} %get-tuple-element.14.row_ref, f32[64,16,384]{2,1,0:T(8,128)} %get-tuple-element.15.band_ref, ...), custom_call_target="tpu_custom_call" | custom-call | tf_op jit(solution)/shard_map/pallas_call | solution.py:314
  55.2 38.2 %shard_map.39 = f32[64,16,1024]{2,1,0:T(8,128)} custom-call(s32[16,128]{1,0:T(8,128)} %broadcast_in_dim.4.margin_ref, s32[16,128]{1,0:T(8,128)} %broadcast_in_dim.5.ramp_ref, f32[64,16,1152]{2,1,0:T(8,128)} %get-tuple-element.14.row_ref, f32[6,16,1152]{2,1,0:T(8,128)} %get-tuple-element.17.low_ref, f32[6,16,1152]{2,1,0:T(8,128)} %get-tuple-element.18.high_ref, ...), custom_call_target="tpu_custom_call" | custom-call | tf_op jit(solution)/shard_map/pallas_call | solution.py:329
